TPU v7x, 256 devices: a whole 4x4x8 slice. The times are simulated.
256 devices in a mesh: loop: 4 (over y_hi, core), inner: 64 (over z, x, y_lo).
Axes of the slice: x: 4, y: 4 (y_hi: 2, y_lo: 2; y = y_hi * 2 + y_lo), z: 8, core: 2. Of those that a mesh axis runs over, the one named last changes fastest.
Arguments:
- snapshots: bfloat16 [65536, 1024], P(('loop', 'inner')), may hold values from -6 to 6
- bins: int32 [65536], replicated, may hold values from 0 to 511, as said below
- pairs: int32 [2048, 2], replicated, may hold values from 0 to 511, as said below
- start_weights: bfloat16 [1024, 32], replicated, may hold values from -0.1875 to 0.1875
Outputs:
- basis: float32 [65536, 96], P(('loop', 'inner'))
- coefficients: float32 [4, 32, 32], replicated
Inputs may be any that keep to these rules, and one draw needn't show every extreme that they name: `bins`: the snapshot in row n has a bin in [r * 8, (r + 1) * 8), where r = (n // 256) mod (64). `pairs`: every row (a, b) has a <= b <= a + 8; every bin is paired with itself.
All inputs are finite; a program needn't handle non-finite values.
Results may differ from a plain program's by a relative error of at most 0.0003.
Values may be sent and summed in bfloat16 or wider, within the bound.
A program may use at most 64 MiB of HBM per device.

v0:
```python
import jax
import jax.numpy as jnp
from jax import lax
from jax.sharding import PartitionSpec as P

STEPS = 2
BINS_COL = 8


def extended(cells, sides, width):
    for axis, dim in sides:
        count = lax.axis_size(axis)
        ends = count - 1
        head = lax.slice_in_dim(cells, 0, width, axis=dim)
        tail = lax.slice_in_dim(cells, cells.shape[dim] - width, cells.shape[dim], axis=dim)
        cells = jnp.concatenate(
            [
                lax.ppermute(tail, axis, [(i, (i + 1) % count) for i in range(ends)]),
                cells,
                lax.ppermute(head, axis, [((i + 1) % count, i) for i in range(ends)]),
            ],
            axis=dim,
        )
    return cells


def matches(values, targets):
    return (values[:, None] == targets[None, :]).astype(jnp.float32)


def local_gram(left, right):
    return jnp.dot(left.T, right, precision=lax.Precision.HIGHEST)


def finish(matrix, gram_total):
    lower_factor = jnp.linalg.cholesky(gram_total)
    result = lax.linalg.triangular_solve(
        lower_factor, matrix, left_side=False, lower=True, transpose_a=True
    )
    return (result, lower_factor.T)


def local(snapshots, bins, pairs, start_weights):
    row_count, features = snapshots.shape
    block_width = start_weights.shape[1]
    n_loop = lax.axis_size("loop")
    n_inner = lax.axis_size("inner")
    column = lax.axis_index("inner")
    group = lax.axis_index("loop")
    bin_grid = jnp.pad(
        bins.reshape(n_loop, n_inner, row_count), ((0, 0), (1, 1), (0, 0)), constant_values=-1
    )
    stacked = lax.all_gather(snapshots[None], "loop", axis=0, tiled=True)
    partner_rows = extended(stacked, (("inner", 1),), row_count)
    tile_rows = partner_rows.reshape(n_loop * 3 * row_count, features)
    tile_bins = lax.dynamic_slice_in_dim(bin_grid, column, 3, 1).reshape(-1)
    my_bins = lax.dynamic_slice_in_dim(bins, (group * n_inner + column) * row_count, row_count)
    bin_base = column * BINS_COL
    my_ids = bin_base + jnp.arange(BINS_COL, dtype=jnp.int32)
    window_ids = bin_base - BINS_COL + jnp.arange(3 * BINS_COL, dtype=jnp.int32)
    left_bins = pairs[:, 0]
    right_bins = pairs[:, 1]
    pair_count = jnp.dot(
        matches(left_bins, my_ids).T,
        matches(right_bins, window_ids),
        precision=lax.Precision.HIGHEST,
    )
    pair_count = pair_count + jnp.dot(
        matches(right_bins, my_ids).T,
        matches(left_bins, window_ids),
        precision=lax.Precision.HIGHEST,
    )
    linked_bins = jnp.where(pair_count > 0.5, 1.0, 0.0).astype(jnp.float32)
    my_hot = matches(my_bins, my_ids)
    row_links = jnp.dot(my_hot, linked_bins)
    mine_wide = snapshots.astype(jnp.float32)
    mine_norms = jnp.sum(mine_wide * mine_wide, axis=1)
    epsilon = features / 3.0
    part_hot = matches(tile_bins, window_ids) * (tile_bins >= 0).astype(jnp.float32)[:, None]
    band_mask = jnp.dot(row_links, part_hot.T)
    part_wide = tile_rows.astype(jnp.float32)
    part_norms = jnp.sum(part_wide * part_wide, axis=1)
    products = lax.dot_general(
        snapshots, tile_rows, (((1,), (1,)), ((), ())), preferred_element_type=jnp.float32
    )
    distance = mine_norms[:, None] + part_norms[None, :] - 2.0 * products
    kept_tiles = [band_mask * jnp.exp(-distance / epsilon)]

    def current_kernel(which):
        return kept_tiles[which]

    degree = jnp.sum(current_kernel(0), axis=1)
    inv_root = lax.rsqrt(degree)
    start_block = jnp.dot(snapshots, start_weights, preferred_element_type=jnp.float32)
    start_total = lax.psum(local_gram(start_block, start_block), ("loop", "inner"))
    current, unused = finish(start_block, start_total)
    basis_blocks = [current]
    coefficients = []
    previous = current
    prev_b = jnp.zeros((block_width, block_width), jnp.float32)
    for lanczos_step in range(STEPS):
        scaled = inv_root[:, None] * current
        vec_stack = lax.all_gather(scaled[None], "loop", axis=0, tiled=True)
        vec_strip = extended(vec_stack, (("inner", 1),), row_count)
        strip = vec_strip.reshape(n_loop * 3 * row_count, block_width)
        total = jnp.dot(current_kernel(0), strip, precision=lax.Precision.HIGHEST)
        image = inv_root[:, None] * total
        projected = lax.psum(local_gram(current, image), ("loop", "inner"))
        image = image - jnp.dot(current, projected, precision=lax.Precision.HIGHEST)
        if lanczos_step > 0:
            image = image - jnp.dot(previous, prev_b.T, precision=lax.Precision.HIGHEST)
        gram_total = lax.psum(local_gram(image, image), ("loop", "inner"))
        following, factor = finish(image, gram_total)
        coefficients.append(projected)
        coefficients.append(factor)
        previous = current
        prev_b = factor
        current = following
        basis_blocks.append(current)
    return (jnp.concatenate(basis_blocks, axis=1), jnp.stack(coefficients))


def solution(mesh):
    in_specs = (P(("loop", "inner"), None), P(), P(), P())
    out_specs = (P(("loop", "inner"), None), P())
    return jax.shard_map(local, mesh=mesh, in_specs=in_specs, out_specs=out_specs, check_vma=False)
```

profile of v0, /device:TPU:1, one launch (start us, length us, event | category | flops | bytes accessed | tf_op | source)
XLA Modules:
  0.0 579.3 jit_solution(10393950573843033094)
XLA Ops:
  9.8 1.3 fusion.49
  11.2 90.2 %psum.35 = f32[32,32]{0,1:T(8,128)S(1)} all-reduce(f32[32,32]{0,1:T(8,128)S(1)} %fusion.50), channel_id=1, replica_groups=mesh['loop'=4,'inner'=64] {'loop','inner'}, use_global_device_ids=true, to_apply=%region_0.1 | all-reduce | flops 1024 | bytes 8192 | tf_op jit(solution)/shard_map/psum | solution.py:95
  101.5 1.3 collective-permute-start.1
  102.8 5.3 collective-permute-start
  108.1 2.9 cholesky.59
  112.4 2.4 custom-call.7
  114.8 1.2 multiply_reduce_fusion.1
  118.8 31.0 %collective-permute-done.1 = bf16[4,256,1024]{2,1,0:T(8,128)(2,1)S(1)} collective-permute-done((bf16[4,256,1024]{2,1,0:T(8,128)(2,1)}, bf16[4,256,1024]{2,1,0:T(8,128)(2,1)S(1)}, u32[]{:S(2)}, u32[]{:S(2)}) %collective-permute-start.1) | collective-permute-done | bytes 2097184 | tf_op jit(solution)/shard_map/ppermute | solution.py:20
  149.8 44.7 %collective-permute-done = bf16[4,256,1024]{2,1,0:T(8,128)(2,1)} collective-permute-done((bf16[4,256,1024]{2,1,0:T(8,128)(2,1)}, bf16[4,256,1024]{2,1,0:T(8,128)(2,1)}, u32[]{:S(2)}, u32[]{:S(2)}) %collective-permute-start) | collective-permute-done | bytes 2097184 | tf_op jit(solution)/shard_map/ppermute | solution.py:18
  194.5 3.6 multiply_reduce_fusion
  198.2 3.5 fusion
  201.7 3.1 fusion.46
  205.0 7.2 %all-gather.1 = f32[1024,32]{0,1:T(8,128)S(1)} all-gather(f32[256,32]{0,1:T(8,128)S(1)} %get-tuple-element.20), channel_id=3, replica_groups=mesh['loop'=4,'inner'=64] {'loop'}, dimensions={0}, use_global_device_ids=true | all-gather | bytes 163840 | tf_op jit(solution)/shard_map/all_gather | solution.py:103
  212.3 1.3 collective-permute-start.3
  213.6 4.8 collective-permute-start.2
  218.4 1.9 collective-permute-done.3
  220.2 3.2 collective-permute-done.2
  223.6 2.8 convolution_multiply_fusion.3
  226.5 80.3 %psum.36 = f32[32,32]{0,1:T(8,128)S(1)} all-reduce(f32[32,32]{0,1:T(8,128)S(1)} %fusion.51), channel_id=1, replica_groups=mesh['loop'=4,'inner'=64] {'loop','inner'}, use_global_device_ids=true, to_apply=%region_6.9 | all-reduce | flops 1024 | bytes 8192 | tf_op jit(solution)/shard_map/psum | solution.py:108
  307.2 75.5 %psum.37 = f32[32,32]{0,1:T(8,128)S(1)} all-reduce(f32[32,32]{0,1:T(8,128)S(1)} %fusion.52), channel_id=1, replica_groups=mesh['loop'=4,'inner'=64] {'loop','inner'}, use_global_device_ids=true, to_apply=%region_7.10 | all-reduce | flops 1024 | bytes 8192 | tf_op jit(solution)/shard_map/psum | solution.py:112
  382.8 2.9 cholesky.70
  387.6 2.4 custom-call.8
  390.3 7.4 %all-gather.2 = f32[1024,32]{0,1:T(8,128)S(1)} all-gather(f32[256,32]{0,1:T(8,128)S(1)} %get-tuple-element.22), channel_id=4, replica_groups=mesh['loop'=4,'inner'=64] {'loop'}, dimensions={0}, use_global_device_ids=true | all-gather | bytes 163840 | tf_op jit(solution)/shard_map/all_gather | solution.py:103
  397.8 1.3 collective-permute-start.5
  399.1 4.0 collective-permute-start.4
  403.1 1.5 collective-permute-done.5
  404.7 2.6 collective-permute-done.4
  407.5 3.5 convolution_multiply_fusion.2
  411.1 76.5 %psum.38 = f32[32,32]{0,1:T(8,128)S(1)} all-reduce(f32[32,32]{0,1:T(8,128)S(1)} %fusion.53), channel_id=1, replica_groups=mesh['loop'=4,'inner'=64] {'loop','inner'}, use_global_device_ids=true, to_apply=%region_8.11 | all-reduce | flops 1024 | bytes 8192 | tf_op jit(solution)/shard_map/psum | solution.py:108
  488.7 75.3 %psum.39 = f32[32,32]{0,1:T(8,128)S(1)} all-reduce(f32[32,32]{0,1:T(8,128)S(1)} %fusion.54), channel_id=1, replica_groups=mesh['loop'=4,'inner'=64] {'loop','inner'}, use_global_device_ids=true, to_apply=%region_9.12 | all-reduce | flops 1024 | bytes 8192 | tf_op jit(solution)/shard_map/psum | solution.py:112
  564.1 2.9 cholesky.81
  568.4 2.4 custom-call.9
  (62 shorter events, 14.6 us)
Async XLA Ops:
  7.2 2.6 copy-start
  7.2 94.4 %all-gather.5.cloned.1.call-start = ((), (), s32[]{:S(2)}) async-start(), calls=%async_computation | async-start | bytes 2621440 | tf_op jit(solution)/shard_map/all_gather | solution.py:53
  101.5 48.3 %collective-permute-start.1 = (bf16[4,256,1024]{2,1,0:T(8,128)(2,1)}, bf16[4,256,1024]{2,1,0:T(8,128)(2,1)S(1)}, u32[]{:S(2)}, u32[]{:S(2)}) collective-permute-start(bf16[4,256,1024]{2,1,0:T(8,128)(2,1)} %bitcast.93), channel_id=1, source_target_pairs={{1,0},{2,1},{3,2},{4,3},{5,4},{6,5},{7,6},{8,7},{9,8},{10,9},{11,1... | collective-permute-start | bytes 6291464 | tf_op jit(solution)/shard_map/ppermute | solution.py:20
  102.8 91.7 %collective-permute-start = (bf16[4,256,1024]{2,1,0:T(8,128)(2,1)}, bf16[4,256,1024]{2,1,0:T(8,128)(2,1)}, u32[]{:S(2)}, u32[]{:S(2)}) collective-permute-start(bf16[4,256,1024]{2,1,0:T(8,128)(2,1)} %bitcast.94), channel_id=1, source_target_pairs={{0,1},{1,2},{2,3},{3,4},{4,5},{5,6},{6,7},{7,8},{8,9},{9,10},{10,1... | collective-permute-start | bytes 6291464 | tf_op jit(solution)/shard_map/ppermute | solution.py:18
  118.8 79.3 %copy-start.1 = (bf16[256,1024]{1,0:T(8,128)(2,1)S(1)}, bf16[256,1024]{1,0:T(8,128)(2,1)}, u32[]{:S(2)}) copy-start(bf16[256,1024]{1,0:T(8,128)(2,1)} %param.7) | copy-start | bytes 1572868
  204.8 185.5 %copy-start.5 = (f32[256]{0:T(256)}, f32[256]{0:T(256)S(1)}, u32[]{:S(2)}) copy-start(f32[256]{0:T(256)S(1)} %rsqrt.7) | copy-start | bytes 3076
  212.3 7.9 %collective-permute-start.3 = (f32[4,256,32]{1,0,2:T(4,128)S(1)}, f32[4,256,32]{1,0,2:T(4,128)S(1)}, u32[]{:S(2)}, u32[]{:S(2)}) collective-permute-start(f32[4,256,32]{1,0,2:T(4,128)S(1)} %reshape.60), channel_id=1, source_target_pairs={{1,0},{2,1},{3,2},{4,3},{5,4},{6,5},{7,6},{8,7},{9,8},{10,9},{11,1... | collective-permute-start | bytes 393224 | tf_op jit(solution)/shard_map/ppermute | solution.py:20
  213.6 9.8 %collective-permute-start.2 = (f32[4,256,32]{1,0,2:T(4,128)S(1)}, f32[4,256,32]{1,0,2:T(4,128)S(1)}, u32[]{:S(2)}, u32[]{:S(2)}) collective-permute-start(f32[4,256,32]{1,0,2:T(4,128)S(1)} %reshape.60), channel_id=1, source_target_pairs={{0,1},{1,2},{2,3},{3,4},{4,5},{5,6},{6,7},{7,8},{8,9},{9,10},{10,1... | collective-permute-start | bytes 393224 | tf_op jit(solution)/shard_map/ppermute | solution.py:18
  306.9 83.4 %copy-start.2 = (f32[32,32]{0,1:T(8,128)}, f32[32,32]{0,1:T(8,128)S(1)}, u32[]{:S(2)}) copy-start(f32[32,32]{0,1:T(8,128)S(1)} %psum.36) | copy-start | bytes 12292
  397.8 173.9 %copy-start.3 = (f32[32,32]{0,1:T(8,128)S(1)}, f32[32,32]{0,1:T(8,128)}, u32[]{:S(2)}) copy-start(f32[32,32]{0,1:T(8,128)} %copy-done.2) | copy-start | bytes 12292
  397.8 173.9 %copy-start.4 = (f32[1,32,32]{1,2,0:T(8,128)S(1)}, f32[1,32,32]{1,2,0:T(8,128)}, u32[]{:S(2)}) copy-start(f32[1,32,32]{1,2,0:T(8,128)} %get-tuple-element.12) | copy-start | bytes 12292
  397.8 6.8 %collective-permute-start.5 = (f32[4,256,32]{1,0,2:T(4,128)S(1)}, f32[4,256,32]{1,0,2:T(4,128)S(1)}, u32[]{:S(2)}, u32[]{:S(2)}) collective-permute-start(f32[4,256,32]{1,0,2:T(4,128)S(1)} %reshape.61), channel_id=1, source_target_pairs={{1,0},{2,1},{3,2},{4,3},{5,4},{6,5},{7,6},{8,7},{9,8},{10,9},{11,1... | collective-permute-start | bytes 393224 | tf_op jit(solution)/shard_map/ppermute | solution.py:20
  399.1 8.2 %collective-permute-start.4 = (f32[4,256,32]{1,0,2:T(4,128)S(1)}, f32[4,256,32]{1,0,2:T(4,128)S(1)}, u32[]{:S(2)}, u32[]{:S(2)}) collective-permute-start(f32[4,256,32]{1,0,2:T(4,128)S(1)} %reshape.61), channel_id=1, source_target_pairs={{0,1},{1,2},{2,3},{3,4},{4,5},{5,6},{6,7},{7,8},{8,9},{9,10},{10,1... | collective-permute-start | bytes 393224 | tf_op jit(solution)/shard_map/ppermute | solution.py:18
Sparse Core Ops, SparseCore 0:
  9.8 33.8 all-gather.4
where the time goes:
time: 581 us; the launch traced here: 579 us
  blocking collectives  413 us (71%)
  waiting for transfers between devices  85.5 us (15%)
  other arithmetic  26.3 us (5%)
  matrix products  18.7 us (3%)
  starting transfers between devices  17.9 us (3%)
  between operations  14.3 us (2%)
    psum x2, blocking collectives, local(): projected = lax.psum(local_gram(current, image), ('loop', 'inner'))  157 us
    psum x2, blocking collectives, local(): gram_total = lax.psum(local_gram(image, image), ('loop', 'inner'))  151 us
    psum x1, blocking collectives, local(): lax.psum(local_gram(start_block, start_block), ('loop', 'inner'))  90.2 us
    ppermute x3, waiting for transfers between devices, extended(): lax.ppermute(tail, axis, [(i, (i + 1) % count) for i in range(ends)])  50.5 us
    ppermute x3, waiting for transfers between devices, extended(): lax.ppermute(head, axis, [((i + 1) % count, i) for i in range(ends)])  34.4 us
    all_gather x2, blocking collectives, local(): vec_stack = lax.all_gather(scaled[None], 'loop', axis=0, tiled=True)  14.7 us
    ppermute x3, starting transfers between devices, extended(): lax.ppermute(tail, axis, [(i, (i + 1) % count) for i in range(ends)])  14 us
  transfers between devices with their start and end apart: 7, of which 6 were waited for; matrix products, arithmetic and copies ran while one was open for 2% of the time, Pallas kernels for 0%

commit v1 on v0

--- a/solution.py
+++ b/solution.py
@@ -92,7 +92,9 @@
     degree = jnp.sum(current_kernel(0), axis=1)
     inv_root = lax.rsqrt(degree)
     start_block = jnp.dot(snapshots, start_weights, preferred_element_type=jnp.float32)
-    start_total = lax.psum(local_gram(start_block, start_block), ("loop", "inner"))
+    x = local_gram(start_block, start_block)
+    parts = lax.all_gather(x, ("loop", "inner"), axis=0, tiled=False)
+    start_total = parts.sum(axis=0)
     current, unused = finish(start_block, start_total)
     basis_blocks = [current]
     coefficients = []

time: 581 us -> 1170 us (2.01)
  waiting for transfers between devices: 85.5 us -> 758 us
  blocking collectives: 413 us -> 331 us
    all_gather x0 -> x1, waiting for transfers between devices: none -> 719 us  [local(): parts = lax.all_gather(x, ('loop', 'inner'), axis=0, tiled=False)]
    psum x1 -> x0, blocking collectives: 90.2 us -> none  [local(): lax.psum(local_gram(start_block, start_block), ('loop', 'inner'))]
    ppermute x3, waiting for transfers between devices: 50.5 us -> 2.64 us  [extended(): lax.ppermute(tail, axis, [(i, (i + 1) % count) for i in range(ends)])]
    all_gather x1, waiting for transfers between devices: 0.01 us -> 32.1 us  [local(): stacked = lax.all_gather(snapshots[None], 'loop', axis=0, tiled=True)]
    ppermute x3, waiting for transfers between devices: 34.4 us -> 3.07 us  [extended(): lax.ppermute(head, axis, [((i + 1) % count, i) for i in range(ends)])]
  transfers between devices with their start and end apart: 7 -> 8, of which waited for: 6 -> 6; matrix products, arithmetic and copies ran while one was open for 2% -> 1% of each run, Pallas kernels for 0% -> 0%
where the time goes in v1:
time: 1170 us
  waiting for transfers between devices  758 us (65%)
  blocking collectives  331 us (28%)
  other arithmetic  28.9 us (2%)
  matrix products  19.3 us (2%)
  starting transfers between devices  17.4 us (1%)
  between operations  14.4 us (1%)
    all_gather x1, waiting for transfers between devices, local(): parts = lax.all_gather(x, ('loop', 'inner'), axis=0, tiled=False)  719 us
    psum x2, blocking collectives, local(): projected = lax.psum(local_gram(current, image), ('loop', 'inner'))  167 us
    psum x2, blocking collectives, local(): gram_total = lax.psum(local_gram(image, image), ('loop', 'inner'))  149 us
    all_gather x1, waiting for transfers between devices, local(): stacked = lax.all_gather(snapshots[None], 'loop', axis=0, tiled=True)  32.1 us
  transfers between devices with their start and end apart: 8, of which 6 were waited for; matrix products, arithmetic and copies ran while one was open for 1% of the time, Pallas kernels for 0%

profile of v1, /device:TPU:1, one launch (start us, length us, event | category | flops | bytes accessed | tf_op | source)
XLA Modules:
  0.0 1172.5 jit_solution(9403220896869877110)
XLA Ops:
  8.0 1.3 fusion.49
  11.2 32.1 %all-gather.9.cloned.1.call-done = bf16[1024,1024]{1,0:T(8,128)(2,1)} async-done(((bf16[256,1024]{1,0:T(8,128)(2,1)}), bf16[1024,1024]{1,0:T(8,128)(2,1)}) %all-gather.9.cloned.1.call-update) | async-done | bytes 2097168 | tf_op jit(solution)/shard_map/all_gather | solution.py:53
  43.3 1.4 collective-permute-start.1
  44.7 5.4 collective-permute-start
  50.9 1.2 multiply_reduce_fusion.1
  54.9 719.2 %all-gather.7.cloned.1.call-done = f32[8192,32]{1,0:T(8,128)} async-done(((f32[32,32]{1,0:T(8,128)}), f32[8192,32]{1,0:T(8,128)}) %all-gather.7.cloned.1.call-update) | async-done | bytes 1048592 | tf_op jit(solution)/shard_map/all_gather | solution.py:96
  774.1 2.5 reduce_sum.36
  776.7 2.9 cholesky.59
  781.0 2.4 custom-call.7
  783.5 3.7 multiply_reduce_fusion
  787.2 3.5 fusion
  790.7 3.1 fusion.46
  794.0 7.8 all-gather.2
  801.9 1.3 collective-permute-start.3
  803.2 4.0 collective-permute-start.2
  807.2 1.5 collective-permute-done.3
  809.8 2.8 convolution_multiply_fusion.3
  812.7 89.1 %psum.28 = f32[32,32]{0,1:T(8,128)S(1)} all-reduce(f32[32,32]{0,1:T(8,128)S(1)} %fusion.51), channel_id=1, replica_groups=mesh['loop'=4,'inner'=64] {'loop','inner'}, use_global_device_ids=true, to_apply=%region_6.9 | all-reduce | flops 1024 | bytes 8192 | tf_op jit(solution)/shard_map/psum | solution.py:110
  902.2 73.4 %psum.29 = f32[32,32]{0,1:T(8,128)S(1)} all-reduce(f32[32,32]{0,1:T(8,128)S(1)} %fusion.52), channel_id=1, replica_groups=mesh['loop'=4,'inner'=64] {'loop','inner'}, use_global_device_ids=true, to_apply=%region_7.10 | all-reduce | flops 1024 | bytes 8192 | tf_op jit(solution)/shard_map/psum | solution.py:114
  975.7 2.9 cholesky.70
  979.3 1.2 fusion.38
  980.4 2.4 custom-call.8
  983.1 7.6 all-gather.3
  990.8 1.3 collective-permute-start.5
  992.1 4.0 collective-permute-start.4
  996.1 1.5 collective-permute-done.5
  997.7 1.8 collective-permute-done.4
  999.6 3.5 convolution_multiply_fusion.2
  1003.3 77.5 %psum.30 = f32[32,32]{0,1:T(8,128)S(1)} all-reduce(f32[32,32]{0,1:T(8,128)S(1)} %fusion.53), channel_id=1, replica_groups=mesh['loop'=4,'inner'=64] {'loop','inner'}, use_global_device_ids=true, to_apply=%region_8.11 | all-reduce | flops 1024 | bytes 8192 | tf_op jit(solution)/shard_map/psum | solution.py:110
  1081.9 75.4 %psum.31 = f32[32,32]{0,1:T(8,128)S(1)} all-reduce(f32[32,32]{0,1:T(8,128)S(1)} %fusion.54), channel_id=1, replica_groups=mesh['loop'=4,'inner'=64] {'loop','inner'}, use_global_device_ids=true, to_apply=%region_9.12 | all-reduce | flops 1024 | bytes 8192 | tf_op jit(solution)/shard_map/psum | solution.py:114
  1157.4 2.9 cholesky.81
  1161.6 2.4 custom-call.9
  (67 shorter events, 15.0 us)
Async XLA Ops:
  7.2 0.8 copy-start
  7.2 36.1 %all-gather.9.cloned.1.call-start = ((), (), s32[]{:S(2)}) async-start(), calls=%async_computation.1 | async-start | bytes 2621440 | tf_op jit(solution)/shard_map/all_gather | solution.py:53
  7.9 766.2 %all-gather.7.cloned.1.call-start = ((), (), s32[]{:S(2)}) async-start(), calls=%async_computation | async-start | bytes 4210688 | tf_op jit(solution)/shard_map/all_gather | solution.py:96
  43.3 740.2 %copy-start.2 = (bf16[1024,1024]{1,0:T(8,128)(2,1)S(1)}, bf16[1024,1024]{1,0:T(8,128)(2,1)}, u32[]{:S(2)}) copy-start(bf16[1024,1024]{1,0:T(8,128)(2,1)} %all-gather.9.cloned.1.call-done) | copy-start | bytes 6291460
  43.3 740.1 %collective-permute-start.1 = (bf16[4,256,1024]{2,1,0:T(8,128)(2,1)}, bf16[4,256,1024]{2,1,0:T(8,128)(2,1)}, u32[]{:S(2)}, u32[]{:S(2)}) collective-permute-start(bf16[4,256,1024]{2,1,0:T(8,128)(2,1)} %bitcast.95), channel_id=1, source_target_pairs={{1,0},{2,1},{3,2},{4,3},{5,4},{6,5},{7,6},{8,7},{9,8},{10,9},{11,1... | collective-permute-start | bytes 6291464 | tf_op jit(solution)/shard_map/ppermute | solution.py:20
  44.7 738.7 %collective-permute-start = (bf16[4,256,1024]{2,1,0:T(8,128)(2,1)}, bf16[4,256,1024]{2,1,0:T(8,128)(2,1)}, u32[]{:S(2)}, u32[]{:S(2)}) collective-permute-start(bf16[4,256,1024]{2,1,0:T(8,128)(2,1)} %bitcast.96), channel_id=1, source_target_pairs={{0,1},{1,2},{2,3},{3,4},{4,5},{5,6},{6,7},{7,8},{8,9},{9,10},{10,1... | collective-permute-start | bytes 6291464 | tf_op jit(solution)/shard_map/ppermute | solution.py:18
  783.4 3.8 copy-start.1
  793.8 189.4 %copy-start.6 = (f32[256]{0:T(256)}, f32[256]{0:T(256)S(1)}, u32[]{:S(2)}) copy-start(f32[256]{0:T(256)S(1)} %rsqrt.7) | copy-start | bytes 3076
  801.9 6.8 collective-permute-start.3
  803.2 6.4 collective-permute-start.2
  901.9 81.3 %copy-start.3 = (f32[32,32]{0,1:T(8,128)}, f32[32,32]{0,1:T(8,128)S(1)}, u32[]{:S(2)}) copy-start(f32[32,32]{0,1:T(8,128)S(1)} %psum.28) | copy-start | bytes 12292
  990.8 174.1 %copy-start.4 = (f32[32,32]{0,1:T(8,128)S(1)}, f32[32,32]{0,1:T(8,128)}, u32[]{:S(2)}) copy-start(f32[32,32]{0,1:T(8,128)} %copy-done.3) | copy-start | bytes 12292
  990.8 174.1 %copy-start.5 = (f32[1,32,32]{1,2,0:T(8,128)S(1)}, f32[1,32,32]{1,2,0:T(8,128)}, u32[]{:S(2)}) copy-start(f32[1,32,32]{1,2,0:T(8,128)} %get-tuple-element.14) | copy-start | bytes 12292
  990.8 6.8 collective-permute-start.5
  992.1 7.3 collective-permute-start.4
Sparse Core Ops, SparseCore 0:
  9.8 33.3 all-gather.8
  45.7 728.3 all-gather.6
